TPU v7x, 32 devices: a whole 2x2x4 slice. The times are simulated.
32 devices in a mesh: ctx: 8 (over z, y), tp: 4 (over x, core).
Axes of the slice: x: 2, y: 2, z: 4, core: 2. Of those that a mesh axis runs over, the one named last changes fastest.
Arguments:
- short_query: bfloat16 [1024, 2048], P('ctx', 'tp'), may hold values from -6 to 6
- short_key: bfloat16 [1024, 2048], P('ctx', 'tp'), may hold values from -6 to 6
- short_value: bfloat16 [1024, 2048], P('ctx', 'tp'), may hold values from -6 to 6
- short_filter: bfloat16 [128, 2048], P(None, 'tp'), may hold values from -0.5 to 0.5
- long_query: bfloat16 [1024, 2048], P('ctx', 'tp'), may hold values from -6 to 6
- long_key: bfloat16 [1024, 2048], P('ctx', 'tp'), may hold values from -6 to 6
- long_filter: bfloat16 [1024, 2048], P('ctx', 'tp'), may hold values from -0.1875 to 0.1875
- out_weight: bfloat16 [2048, 2048], P('tp'), may hold values from -0.125 to 0.125
- out_grad: bfloat16 [1024, 2048], P('ctx', 'tp'), may hold values from -6 to 6
Outputs:
- short_query_grad: bfloat16 [1024, 2048], P('ctx', 'tp')
- short_key_grad: bfloat16 [1024, 2048], P('ctx', 'tp')
- short_value_grad: bfloat16 [1024, 2048], P('ctx', 'tp')
- short_filter_grad: bfloat16 [128, 2048], P(None, 'tp')
- long_query_grad: bfloat16 [1024, 2048], P('ctx', 'tp')
- long_key_grad: bfloat16 [1024, 2048], P('ctx', 'tp')
- long_filter_grad: bfloat16 [1024, 2048], P('ctx', 'tp')
All inputs are finite; a program needn't handle non-finite values.
Results may differ from a plain program's by a relative error of at most 0.015.
Values may be sent and summed in bfloat16 or wider, within the bound.
A program may use at most 64 MiB of HBM per device.

v0:
```python
import math

import jax
import jax.numpy as jnp
from jax import lax
from jax.sharding import PartitionSpec as P


def passed_along(block, axis, distance):
    devices = range(lax.axis_size(axis))
    route = [(i - distance, i) for i in devices if i - distance in devices]
    return lax.ppermute(block, axis, route)


def angle_tables(blocks, inner):
    size_one = 2 * blocks
    whole = size_one * inner
    first = (
        lax.broadcasted_iota(jnp.int32, (size_one, blocks), 0)
        * lax.broadcasted_iota(jnp.int32, (size_one, blocks), 1)
        % size_one
    )
    phase_one = first.astype(jnp.float32) * (2.0 * math.pi / size_one)
    twist = (
        lax.broadcasted_iota(jnp.int32, (size_one, inner), 0)
        * lax.broadcasted_iota(jnp.int32, (size_one, inner), 1)
        % whole
    )
    phase_twist = twist.astype(jnp.float32) * (2.0 * math.pi / whole)
    second = (
        lax.broadcasted_iota(jnp.int32, (inner, inner), 0)
        * lax.broadcasted_iota(jnp.int32, (inner, inner), 1)
        % inner
    )
    phase_two = second.astype(jnp.float32) * (2.0 * math.pi / inner)
    return (
        jnp.cos(phase_one),
        jnp.sin(phase_one),
        jnp.cos(phase_twist)[:, None, :],
        jnp.sin(phase_twist)[:, None, :],
        jnp.cos(phase_two),
        jnp.sin(phase_two),
        whole,
    )


def spectrum(values, tables):
    cos_one, sin_one, cos_twist, sin_twist, cos_two, sin_two, whole = tables
    highest = lax.Precision.HIGHEST
    real_a = jnp.einsum("kn,ncm->kcm", cos_one, values, precision=highest)
    imag_a = -jnp.einsum("kn,ncm->kcm", sin_one, values, precision=highest)
    real_b = real_a * cos_twist + imag_a * sin_twist
    imag_b = imag_a * cos_twist - real_a * sin_twist
    real_c = jnp.einsum("kcm,mq->kcq", real_b, cos_two, precision=highest) + jnp.einsum(
        "kcm,mq->kcq", imag_b, sin_two, precision=highest
    )
    imag_c = jnp.einsum("kcm,mq->kcq", imag_b, cos_two, precision=highest) - jnp.einsum(
        "kcm,mq->kcq", real_b, sin_two, precision=highest
    )
    return (real_c, imag_c)


def restore(real_in, imag_in, tables, both):
    cos_one, sin_one, cos_twist, sin_twist, cos_two, sin_two, whole = tables
    highest = lax.Precision.HIGHEST
    real_p = jnp.einsum("kcq,qm->kcm", real_in, cos_two, precision=highest) - jnp.einsum(
        "kcq,qm->kcm", imag_in, sin_two, precision=highest
    )
    imag_p = jnp.einsum("kcq,qm->kcm", imag_in, cos_two, precision=highest) + jnp.einsum(
        "kcq,qm->kcm", real_in, sin_two, precision=highest
    )
    real_q = real_p * cos_twist - imag_p * sin_twist
    imag_q = imag_p * cos_twist + real_p * sin_twist
    real_out = (
        jnp.einsum("kn,kcm->ncm", cos_one, real_q, precision=highest)
        - jnp.einsum("kn,kcm->ncm", sin_one, imag_q, precision=highest)
    ) / whole
    if both:
        imag_out = (
            jnp.einsum("kn,kcm->ncm", cos_one, imag_q, precision=highest)
            + jnp.einsum("kn,kcm->ncm", sin_one, real_q, precision=highest)
        ) / whole
        return (real_out, imag_out)
    return real_out


def spectral(product, gated, filter_in):
    blocks, count, inner = product.shape
    tables = angle_tables(blocks, inner)
    real_u, imag_u = spectrum(product.astype(jnp.float32), tables)
    real_g, imag_g = spectrum(gated.astype(jnp.float32), tables)
    real_h, imag_h = spectrum(filter_in.astype(jnp.float32), tables)
    real_pair = real_h * real_u - imag_h * imag_u - real_h * imag_g + imag_h * real_g
    imag_pair = real_h * imag_u + imag_h * real_u + real_h * real_g + imag_h * imag_g
    conv_part, back_part = restore(real_pair, imag_pair, tables, True)
    filter_part = restore(
        real_u * real_g + imag_u * imag_g, real_u * imag_g - imag_u * real_g, tables, False
    )
    return (conv_part, back_part, filter_part)


def tap_sum(extended, weights, token_rows, causal):
    filter_taps, channels = weights.shape

    def group_step(group, total):
        for inner in range(8):
            place = group * 8 + inner
            weight_row = lax.dynamic_index_in_dim(weights, place, 0, keepdims=False).astype(
                jnp.float32
            )
            start = filter_taps - 1 - place if causal else place
            shifted = lax.dynamic_slice_in_dim(extended, start, token_rows, 0).astype(jnp.float32)
            total = total + weight_row[None, :] * shifted
        return total

    return lax.fori_loop(
        0, filter_taps // 8, group_step, jnp.zeros((token_rows, channels), jnp.float32)
    )


def filter_terms(extended, grads, filter_taps):
    token_rows, channels = grads.shape

    def group_terms(group):
        partials = []
        for inner in range(8):
            place = group * 8 + inner
            shifted = lax.dynamic_slice_in_dim(
                extended, filter_taps - 1 - place, token_rows, 0
            ).astype(jnp.float32)
            partials.append(jnp.sum(grads * shifted, axis=0))
        return jnp.stack(partials)

    stacked = lax.map(group_terms, jnp.arange(filter_taps // 8, dtype=jnp.int32))
    return stacked.reshape(filter_taps, channels)


def body(
    short_query,
    short_key,
    short_value,
    short_filter,
    long_query,
    long_key,
    long_filter,
    out_weight,
    out_grad,
):
    token_rows, channels = short_query.shape
    groups = lax.axis_size("ctx")
    seq_len = token_rows * groups
    scaling = 1.0 / math.sqrt(seq_len)
    filter_taps = short_filter.shape[0]
    product_one = (short_key.astype(jnp.float32) * short_value.astype(jnp.float32)).astype(
        jnp.bfloat16
    )
    before = passed_along(product_one[token_rows - (filter_taps - 1) :], "ctx", 1)
    extended_prod = jnp.concatenate([before, product_one], axis=0)
    short_mix = tap_sum(extended_prod, short_filter, token_rows, True)
    mixed = (short_query.astype(jnp.float32) * short_mix).astype(jnp.bfloat16)
    grad_two = lax.dot_general(
        lax.all_gather(out_grad, "tp", axis=1, tiled=True),
        out_weight,
        (((1,), (1,)), ((), ())),
        preferred_element_type=jnp.float32,
    ).astype(jnp.bfloat16)

    def to_channels(values):
        return values.T.reshape(groups, channels // groups, token_rows)

    def to_tokens(values):
        return values.reshape(channels, token_rows).T

    product_two = (long_key.astype(jnp.float32) * mixed.astype(jnp.float32)).astype(jnp.bfloat16)
    gated_two = (grad_two.astype(jnp.float32) * long_query.astype(jnp.float32)).astype(jnp.bfloat16)
    conv_part, back_part, filter_part = spectral(
        lax.all_to_all(to_channels(product_two), "ctx", split_axis=0, concat_axis=0, tiled=True),
        lax.all_to_all(to_channels(gated_two), "ctx", split_axis=0, concat_axis=0, tiled=True),
        lax.all_to_all(to_channels(long_filter), "ctx", split_axis=0, concat_axis=0, tiled=True),
    )
    long_mix = lax.all_to_all(conv_part, "ctx", split_axis=0, concat_axis=0, tiled=True)
    back_two = lax.all_to_all(back_part, "ctx", split_axis=0, concat_axis=0, tiled=True)
    filter_two = lax.all_to_all(filter_part, "ctx", split_axis=0, concat_axis=0, tiled=True)
    long_mix = to_tokens(long_mix)
    back_two = to_tokens(back_two)
    filter_two = to_tokens(filter_two)
    long_query_grad = (grad_two.astype(jnp.float32) * long_mix).astype(jnp.bfloat16)
    long_key_grad = (back_two * mixed.astype(jnp.float32)).astype(jnp.bfloat16)
    mixed_grad = (back_two * long_key.astype(jnp.float32)).astype(jnp.bfloat16)
    long_filter_grad = (filter_two * scaling).astype(jnp.bfloat16)
    gated_one = (mixed_grad.astype(jnp.float32) * short_query.astype(jnp.float32)).astype(
        jnp.bfloat16
    )
    short_query_grad = (mixed_grad.astype(jnp.float32) * short_mix).astype(jnp.bfloat16)
    after = passed_along(gated_one[: filter_taps - 1], "ctx", -1)
    extended_grad = jnp.concatenate([gated_one, after], axis=0)
    back_one = tap_sum(extended_grad, short_filter, token_rows, False)
    short_key_grad = (back_one * short_value.astype(jnp.float32)).astype(jnp.bfloat16)
    short_value_grad = (back_one * short_key.astype(jnp.float32)).astype(jnp.bfloat16)
    local_terms = filter_terms(extended_prod, gated_one.astype(jnp.float32), filter_taps)
    filter_one = lax.psum(local_terms, "ctx")
    short_filter_grad = (filter_one * scaling).astype(jnp.bfloat16)
    return (
        short_query_grad,
        short_key_grad,
        short_value_grad,
        short_filter_grad,
        long_query_grad,
        long_key_grad,
        long_filter_grad,
    )


def solution(mesh):
    in_specs = (
        P("ctx", "tp"),
        P("ctx", "tp"),
        P("ctx", "tp"),
        P(None, "tp"),
        P("ctx", "tp"),
        P("ctx", "tp"),
        P("ctx", "tp"),
        P("tp", None),
        P("ctx", "tp"),
    )
    out_specs = (
        P("ctx", "tp"),
        P("ctx", "tp"),
        P("ctx", "tp"),
        P(None, "tp"),
        P("ctx", "tp"),
        P("ctx", "tp"),
        P("ctx", "tp"),
    )
    return jax.shard_map(body, mesh=mesh, in_specs=in_specs, out_specs=out_specs, check_vma=False)
```

profile of v0, /device:TPU:0, one launch (start us, length us, event | category | flops | bytes accessed | tf_op | source)
XLA Modules:
  0.0 284.4 jit_solution(5486924148167031176)
XLA Ops:
  7.2 1.2 fusion.74
  9.0 5.5 %collective-permute-start = (bf16[127,512]{1,0:T(8,128)(2,1)}, bf16[127,512]{1,0:T(8,128)(2,1)}, u32[]{:S(2)}, u32[]{:S(2)}) collective-permute-start(bf16[127,512]{1,0:T(8,128)(2,1)} %slice.8), channel_id=1, source_target_pairs={{0,4},{4,8},{8,12},{12,16},{16,20},{20,24},{24,28},{1,5},{5,9},{9,... | collective-permute-start | bytes 390152 | tf_op jit(solution)/shard_map/ppermute | solution.py:12
  14.6 7.4 %all_gather.3 = bf16[128,2048]{1,0:T(8,128)(2,1)S(1)} all-gather(bf16[128,512]{1,0:T(8,128)(2,1)} %param.23), channel_id=1, replica_groups=mesh['ctx'=8,'tp'=4] {'tp'}, dimensions={1}, use_global_device_ids=true | all-gather | bytes 655360 | tf_op jit(solution)/shard_map/all_gather | solution.py:162
  24.3 4.2 %all-to-all-start.2 = ((bf16[8,64,128]{2,1,0:T(8,128)(2,1)}), bf16[8,64,128]{2,1,0:T(8,128)(2,1)S(1)}, u32[]{:S(2)}, u32[]{:S(2)}) async-start(bf16[8,64,128]{2,1,0:T(8,128)(2,1)} %bitcast.34), calls=%async_computation.2 | async-start | bytes 262144 | tf_op jit(solution)/shard_map/all_to_all | solution.py:178
  30.6 24.5 %while.47 = (s32[]{:T(128)}, f32[128,512]{1,0:T(8,128)S(1)}, bf16[128,512]{1,0:T(8,128)(2,1)}, bf16[255,512]{1,0:T(8,128)(2,1)S(1)}, s32[]{:T(128)}, /*index=5*/...) while((s32[]{:T(128)}, f32[128,512]{1,0:T(8,128)S(1)}, ...), condition=%wide.region_1.2_spmd.clone, body=%wide.region_0.1_spmd.clone.sunk | while | flops 1642563 | bytes 1614839 | solution.py:116
  56.6 6.0 %all-to-all-start = ((bf16[8,64,128]{2,1,0:T(8,128)(2,1)}), bf16[8,64,128]{2,1,0:T(8,128)(2,1)S(1)}, u32[]{:S(2)}, u32[]{:S(2)}) async-start(bf16[8,64,128]{2,1,0:T(8,128)(2,1)} %bitcast.27), calls=%async_computation | async-start | bytes 262144 | tf_op jit(solution)/shard_map/all_to_all | solution.py:179
  62.6 1.4 convolution_negate_fusion
  64.0 2.2 fusion.89
  66.2 3.8 %all-to-all-done = bf16[8,64,128]{2,1,0:T(8,128)(2,1)S(1)} async-done(((bf16[8,64,128]{2,1,0:T(8,128)(2,1)}), bf16[8,64,128]{2,1,0:T(8,128)(2,1)S(1)}, u32[]{:S(2)}, u32[]{:S(2)}) %all-to-all-start) | async-done | bytes 131104 | tf_op jit(solution)/shard_map/all_to_all | solution.py:179
  70.0 3.6 %all-to-all-start.1 = ((bf16[8,64,128]{2,1,0:T(8,128)(2,1)}), bf16[8,64,128]{2,1,0:T(8,128)(2,1)S(1)}, u32[]{:S(2)}, u32[]{:S(2)}) async-start(bf16[8,64,128]{2,1,0:T(8,128)(2,1)} %bitcast.227), calls=%async_computation.1 | async-start | bytes 262144 | tf_op jit(solution)/shard_map/all_to_all | solution.py:177
  73.5 1.3 convolution_negate_fusion.2
  74.8 1.3 fusion.95
  76.1 4.5 %all-to-all-done.1 = bf16[8,64,128]{2,1,0:T(8,128)(2,1)S(1)} async-done(((bf16[8,64,128]{2,1,0:T(8,128)(2,1)}), bf16[8,64,128]{2,1,0:T(8,128)(2,1)S(1)}, u32[]{:S(2)}, u32[]{:S(2)}) %all-to-all-start.1) | async-done | bytes 131104 | tf_op jit(solution)/shard_map/all_to_all | solution.py:177
  81.1 2.1 multiply_add_fusion.5
  93.1 1.5 multiply_add_fusion
  100.4 4.1 %all-to-all-start.5 = ((f32[8,64,128]{2,1,0:T(8,128)}), f32[8,64,128]{2,1,0:T(8,128)}, u32[]{:S(2)}, u32[]{:S(2)}) async-start(f32[8,64,128]{2,1,0:T(8,128)} %copy.113), calls=%async_computation.5 | async-start | bytes 524288 | tf_op jit(solution)/shard_map/all_to_all | solution.py:183
  107.7 1.1 convolution_subtract_fusion.1
  110.4 2.3 all-to-all-done.5
  112.7 4.3 %all-to-all-start.4 = ((f32[8,64,128]{2,1,0:T(8,128)}), f32[8,64,128]{2,1,0:T(8,128)}, u32[]{:S(2)}, u32[]{:S(2)}) async-start(f32[8,64,128]{2,1,0:T(8,128)} %copy.107), calls=%async_computation.4 | async-start | bytes 524288 | tf_op jit(solution)/shard_map/all_to_all | solution.py:181
  118.7 6.3 %all-to-all-done.4 = f32[8,64,128]{2,1,0:T(8,128)} async-done(((f32[8,64,128]{2,1,0:T(8,128)}), f32[8,64,128]{2,1,0:T(8,128)}, u32[]{:S(2)}, u32[]{:S(2)}) %all-to-all-start.4) | async-done | bytes 262176 | tf_op jit(solution)/shard_map/all_to_all | solution.py:181
  125.0 4.1 %all-to-all-start.3 = ((f32[8,64,128]{2,1,0:T(8,128)}), f32[8,64,128]{2,1,0:T(8,128)}, u32[]{:S(2)}, u32[]{:S(2)}) async-start(f32[8,64,128]{2,1,0:T(8,128)} %copy.103), calls=%async_computation.3 | async-start | bytes 524288 | tf_op jit(solution)/shard_map/all_to_all | solution.py:182
  130.9 1.8 copy.108
  132.7 4.6 %all-to-all-done.3 = f32[8,64,128]{2,1,0:T(8,128)} async-done(((f32[8,64,128]{2,1,0:T(8,128)}), f32[8,64,128]{2,1,0:T(8,128)}, u32[]{:S(2)}, u32[]{:S(2)}) %all-to-all-start.3) | async-done | bytes 262176 | tf_op jit(solution)/shard_map/all_to_all | solution.py:182
  137.3 1.7 fusion.77
  139.7 68.0 %while.46 = (s32[]{:T(128)}, f32[16,8,512]{2,1,0:T(8,128)}, s32[16]{0:T(128)}, bf16[255,512]{1,0:T(8,128)(2,1)S(1)}, f32[128,512]{1,0:T(8,128)S(1)}, /*index=5*/...) while((s32[]{:T(128)}, f32[16,8,512]{2,1,0:T(8,128)}, ...), condition=%wide.region_13.14_spmd, body=%wide.region_4.13_spmd.sunk | while | flops 1568810 | bytes 1393817 | solution.py:134
  139.7 1.2 dynamic_slice.526
  144.0 1.2 dynamic_slice.526
  148.2 1.2 dynamic_slice.526
  152.5 1.2 dynamic_slice.526
  156.7 1.2 dynamic_slice.526
  160.9 1.2 dynamic_slice.526
  165.2 1.2 dynamic_slice.526
  169.4 1.2 dynamic_slice.526
  173.7 1.2 dynamic_slice.526
  177.9 1.2 dynamic_slice.526
  182.2 1.2 dynamic_slice.526
  186.4 1.2 dynamic_slice.526
  190.7 1.2 dynamic_slice.526
  194.9 1.2 dynamic_slice.526
  199.2 1.2 dynamic_slice.526
  203.4 1.2 dynamic_slice.526
  207.7 1.3 collective-permute-start.1
  209.0 1.7 copy.114
  210.6 1.7 copy.115
  213.0 2.3 collective-permute-done.1
  215.5 24.4 %while.48 = (s32[]{:T(128)}, f32[128,512]{1,0:T(8,128)S(1)}, bf16[128,512]{1,0:T(8,128)(2,1)}, bf16[255,512]{1,0:T(8,128)(2,1)S(1)}, s32[]{:T(128)}, /*index=5*/...) while((s32[]{:T(128)}, f32[128,512]{1,0:T(8,128)S(1)}, ...), condition=%wide.region_3.4_spmd.clone, body=%wide.region_2.3_spmd.clone.sunk | while | flops 1642547 | bytes 1614719 | solution.py:116
  240.7 35.3 %all-reduce.2.cloned.1.call-done = f32[128,512]{1,0:T(8,128)} async-done(((f32[128,512]{1,0:T(8,128)}), f32[128,512]{1,0:T(8,128)}) %all-reduce.2.cloned.1.call-update) | async-done | bytes 262160 | tf_op jit(solution)/shard_map/psum | solution.py:201
  276.0 1.6 multiply_convert_fusion.1
  (200 shorter events, 115.5 us)
Async XLA Ops:
  7.2 14.8 %copy-start = (bf16[512,2048]{1,0:T(8,128)(2,1)S(1)}, bf16[512,2048]{1,0:T(8,128)(2,1)}, u32[]{:S(2)}) copy-start(bf16[512,2048]{1,0:T(8,128)(2,1)} %param.22) | copy-start | bytes 6291460
  7.2 16.3 %copy-start.16 = (bf16[128,512]{1,0:T(8,128)(2,1)S(1)}, bf16[128,512]{1,0:T(8,128)(2,1)}, u32[]{:S(2)}) copy-start(bf16[128,512]{1,0:T(8,128)(2,1)} %param.19) | copy-start | bytes 393220
  9.0 20.6 %collective-permute-start = (bf16[127,512]{1,0:T(8,128)(2,1)}, bf16[127,512]{1,0:T(8,128)(2,1)}, u32[]{:S(2)}, u32[]{:S(2)}) collective-permute-start(bf16[127,512]{1,0:T(8,128)(2,1)} %slice.8), channel_id=1, source_target_pairs={{0,4},{4,8},{8,12},{12,16},{16,20},{20,24},{24,28},{1,5},{5,9},{9,... | collective-permute-start | bytes 390152 | tf_op jit(solution)/shard_map/ppermute | solution.py:12
  21.9 6.6 %copy-start.13 = (bf16[128,512]{1,0:T(8,128)(2,1)S(1)}, bf16[128,512]{1,0:T(8,128)(2,1)}, u32[]{:S(2)}) copy-start(bf16[128,512]{1,0:T(8,128)(2,1)} %param.20) | copy-start | bytes 393220
  21.9 6.7 %copy-start.14 = (bf16[128,512]{1,0:T(8,128)(2,1)S(1)}, bf16[128,512]{1,0:T(8,128)(2,1)}, u32[]{:S(2)}) copy-start(bf16[128,512]{1,0:T(8,128)(2,1)} %param.15) | copy-start | bytes 393220
  21.9 6.8 %copy-start.15 = (bf16[128,512]{1,0:T(8,128)(2,1)S(1)}, bf16[128,512]{1,0:T(8,128)(2,1)}, u32[]{:S(2)}) copy-start(bf16[128,512]{1,0:T(8,128)(2,1)} %param.21) | copy-start | bytes 393220
  22.8 0.7 copy-start.5
  24.3 31.7 %all-to-all-start.2 = ((bf16[8,64,128]{2,1,0:T(8,128)(2,1)}), bf16[8,64,128]{2,1,0:T(8,128)(2,1)S(1)}, u32[]{:S(2)}, u32[]{:S(2)}) async-start(bf16[8,64,128]{2,1,0:T(8,128)(2,1)} %bitcast.34), calls=%async_computation.2 | async-start | bytes 262144 | tf_op jit(solution)/shard_map/all_to_all | solution.py:178
  28.8 26.4 %copy-start.7 = (bf16[128,512]{0,1:T(8,128)(2,1)}, bf16[128,512]{0,1:T(8,128)(2,1)S(1)}, u32[]{:S(2)}) copy-start(bf16[128,512]{0,1:T(8,128)(2,1)S(1)} %copy.82) | copy-start | bytes 393220
  55.2 25.9 %copy-start.3 = (f32[128,512]{0,1:T(8,128)}, f32[128,512]{0,1:T(8,128)S(1)}, u32[]{:S(2)}) copy-start(f32[128,512]{0,1:T(8,128)S(1)} %copy.83) | copy-start | bytes 786436
  56.0 0.7 copy-start.9
  56.6 13.3 %all-to-all-start = ((bf16[8,64,128]{2,1,0:T(8,128)(2,1)}), bf16[8,64,128]{2,1,0:T(8,128)(2,1)S(1)}, u32[]{:S(2)}, u32[]{:S(2)}) async-start(bf16[8,64,128]{2,1,0:T(8,128)(2,1)} %bitcast.27), calls=%async_computation | async-start | bytes 262144 | tf_op jit(solution)/shard_map/all_to_all | solution.py:179
  70.0 10.7 %all-to-all-start.1 = ((bf16[8,64,128]{2,1,0:T(8,128)(2,1)}), bf16[8,64,128]{2,1,0:T(8,128)(2,1)S(1)}, u32[]{:S(2)}, u32[]{:S(2)}) async-start(bf16[8,64,128]{2,1,0:T(8,128)(2,1)} %bitcast.227), calls=%async_computation.1 | async-start | bytes 262144 | tf_op jit(solution)/shard_map/all_to_all | solution.py:177
  94.5 9.9 %copy-start.1 = (f32[16,64,128]{2,1,0:T(8,128)}, f32[16,64,128]{2,1,0:T(8,128)S(1)}, u32[]{:S(2)}) copy-start(f32[16,64,128]{2,1,0:T(8,128)S(1)} %get-tuple-element.488) | copy-start | bytes 1572868
  100.4 12.3 %all-to-all-start.5 = ((f32[8,64,128]{2,1,0:T(8,128)}), f32[8,64,128]{2,1,0:T(8,128)}, u32[]{:S(2)}, u32[]{:S(2)}) async-start(f32[8,64,128]{2,1,0:T(8,128)} %copy.113), calls=%async_computation.5 | async-start | bytes 524288 | tf_op jit(solution)/shard_map/all_to_all | solution.py:183
  105.5 2.1 copy-start.2
  112.7 12.3 %all-to-all-start.4 = ((f32[8,64,128]{2,1,0:T(8,128)}), f32[8,64,128]{2,1,0:T(8,128)}, u32[]{:S(2)}, u32[]{:S(2)}) async-start(f32[8,64,128]{2,1,0:T(8,128)} %copy.107), calls=%async_computation.4 | async-start | bytes 524288 | tf_op jit(solution)/shard_map/all_to_all | solution.py:181
  117.9 19.4 %copy-start.4 = (f32[128,512]{0,1:T(8,128)S(1)}, f32[128,512]{0,1:T(8,128)}, u32[]{:S(2)}) copy-start(f32[128,512]{0,1:T(8,128)} %copy-done.3) | copy-start | bytes 786436
  117.9 19.4 %copy-start.8 = (bf16[128,512]{0,1:T(8,128)(2,1)S(1)}, bf16[128,512]{0,1:T(8,128)(2,1)}, u32[]{:S(2)}) copy-start(bf16[128,512]{0,1:T(8,128)(2,1)} %copy-done.7) | copy-start | bytes 393220
  125.0 12.3 %all-to-all-start.3 = ((f32[8,64,128]{2,1,0:T(8,128)}), f32[8,64,128]{2,1,0:T(8,128)}, u32[]{:S(2)}, u32[]{:S(2)}) async-start(f32[8,64,128]{2,1,0:T(8,128)} %copy.103), calls=%async_computation.3 | async-start | bytes 524288 | tf_op jit(solution)/shard_map/all_to_all | solution.py:182
  129.1 146.9 %all-reduce.2.cloned.1.call-start = ((), (), s32[]{:S(2)}) async-start(), calls=%async_computation.6 | async-start | bytes 524288 | tf_op jit(solution)/shard_map/psum | solution.py:201
  139.7 72.6 %copy-start.6 = (f32[128,512]{1,0:T(8,128)S(1)}, f32[128,512]{1,0:T(8,128)}, u32[]{:S(2)}) copy-start(f32[128,512]{1,0:T(8,128)} %copy-done.5) | copy-start | bytes 786436
  139.7 72.6 %copy-start.10 = (f32[512,128]{0,1:T(8,128)S(1)}, f32[512,128]{0,1:T(8,128)}, u32[]{:S(2)}) copy-start(f32[512,128]{0,1:T(8,128)} %copy.108) | copy-start | bytes 786436
  207.7 7.6 %collective-permute-start.1 = (bf16[127,512]{0,1:T(8,128)(2,1)S(1)}, bf16[127,512]{0,1:T(8,128)(2,1)S(1)}, u32[]{:S(2)}, u32[]{:S(2)}) collective-permute-start(bf16[127,512]{0,1:T(8,128)(2,1)S(1)} %bitcast.226), channel_id=1, source_target_pairs={{4,0},{8,4},{12,8},{16,12},{20,16},{24,20},{28,24},{5,1},{9,5},{13... | collective-permute-start | bytes 390152 | tf_op jit(solution)/shard_map/ppermute | solution.py:12
  215.4 24.4 %copy-start.11 = (bf16[128,512]{1,0:T(8,128)(2,1)S(1)}, bf16[128,512]{1,0:T(8,128)(2,1)}, u32[]{:S(2)}) copy-start(bf16[128,512]{1,0:T(8,128)(2,1)} %param.17) | copy-start | bytes 393220
  215.5 24.4 %copy-start.12 = (bf16[128,512]{1,0:T(8,128)(2,1)S(1)}, bf16[128,512]{1,0:T(8,128)(2,1)}, u32[]{:S(2)}) copy-start(bf16[128,512]{1,0:T(8,128)(2,1)} %param.16) | copy-start | bytes 393220
Sparse Core Ops, SparseCore 0:
  207.8 68.1 all-reduce.1
where the time goes:
time: 288 us; the launch traced here: 284 us
  other arithmetic  68.9 us (24%)
  waiting for transfers between devices  59.1 us (21%)
  local copies, waits for them, and re-layouts  53.9 us (19%)
  starting transfers between devices  33.1 us (11%)
  matrix products  31.8 us (11%)
  loops' own time  15.7 us (5%)
  between operations  14.6 us (5%)
  blocking collectives  7.37 us (3%)
    psum x1, waiting for transfers between devices, body(): filter_one = lax.psum(local_terms, 'ctx')  35.3 us
    mul x32, other arithmetic, group_step(): total = total + weight_row[None, :] * shifted  32.7 us
    dynamic_slice x16, local copies, waits for them, and re-layouts, filter_terms(): lax.map(group_terms, jnp.arange(filter_taps // 8, dtype=jnp.int32))  18.9 us
    reduce_sum x16, other arithmetic, group_terms(): partials.append(jnp.sum(grads * shifted, axis=0))  15.9 us
    another operation x16, local copies, waits for them, and re-layouts, group_terms(): return jnp.stack(partials)  12.5 us
    add x32, other arithmetic, group_step(): total = total + weight_row[None, :] * shifted  11.6 us
    another operation x1, loops' own time, filter_terms(): lax.map(group_terms, jnp.arange(filter_taps // 8, dtype=jnp.int32))  11.1 us
    dynamic_update_slice x16, local copies, waits for them, and re-layouts, filter_terms(): lax.map(group_terms, jnp.arange(filter_taps // 8, dtype=jnp.int32))  9.67 us
  transfers between devices with their start and end apart: 9, of which 7 were waited for; matrix products, arithmetic and copies ran while one was open for 25% of the time, Pallas kernels for 0%

commit v1 on v0

--- a/solution.py
+++ b/solution.py
@@ -1,9 +1,20 @@
+import functools
 import math
 
 import jax
 import jax.numpy as jnp
+import ml_dtypes
+import numpy as np
 from jax import lax
+from jax.experimental import pallas as pl
+from jax.experimental.pallas import tpu as pltpu
 from jax.sharding import PartitionSpec as P
+
+MESH = pl.DeviceIdType.MESH
+BF16 = jnp.bfloat16
+F32 = jnp.float32
+LONGEST_DENSE = 2048
+PARTS = ("prod", "gates", "grad", "smix", "lmix", "filt", "back", "bone", "taps")
 
 
 def passed_along(block, axis, distance):
@@ -135,7 +146,7 @@
     return stacked.reshape(filter_taps, channels)
 
 
-def body(
+def general_body(
     short_query,
     short_key,
     short_value,
@@ -211,6 +222,357 @@
     )
 
 
+def wave_tables(seq_len):
+    time = np.arange(seq_len, dtype=np.int64)[:, None]
+    odd = 2 * np.arange(seq_len, dtype=np.int64)[None, :] + 1
+    phase = (time * odd % (4 * seq_len)).astype(np.float64) * (math.pi / (2 * seq_len))
+    forward = np.concatenate([np.cos(phase), np.sin(phase)], axis=1)
+    return (
+        forward.astype(ml_dtypes.bfloat16),
+        np.ascontiguousarray(forward.T).astype(ml_dtypes.bfloat16),
+    )
+
+
+def dot(a, b):
+    return jnp.dot(a, b, preferred_element_type=F32)
+
+
+def flipped(block):
+    return block.astype(F32).T.astype(BF16)
+
+
+def operator_kernel(
+    n, m,
+    sq, sk, sv, sf, lq, lk, lf, og, weight, forward, inverse,
+    grad_out, smix_out, lmix_out, filt_out, back_out, bone_out, taps_out,
+    weight_v, fwd, inv, og_rx, tx_prod, tx_gates, tx_grad, rx_prod, rx_gates, rx_grad,
+    tx_smix, tx_lmix, tx_filt, tx_back, tx_bone, tx_taps, filter_t, signals, smix,
+    spec_prod, spec_sf, spec_u, spec_h, waves, load_sem, og_send, og_recv, send, recv,
+):
+    me = lax.axis_index("ctx")
+    col = lax.axis_index("tp")
+    rows, chans = sq.shape
+    cb = chans // n
+    taps = sf.shape[0]
+    seq = rows * n
+    tile = 2 * rows
+    kt = 256
+
+    loads = []
+    for place, (source, target) in enumerate(((weight, weight_v), (forward, fwd), (inverse, inv))):
+        load = pltpu.make_async_copy(source, target, load_sem.at[place])
+        load.start()
+        loads.append(load)
+
+    barrier = pltpu.get_barrier_semaphore()
+    for d in range(1, n):
+        pl.semaphore_signal(
+            barrier, inc=1, device_id=(lax.rem(me + d, n), col), device_id_type=MESH
+        )
+    for d in range(1, m):
+        pl.semaphore_signal(
+            barrier, inc=1, device_id=(me, lax.rem(col + d, m)), device_id_type=MESH
+        )
+    pl.semaphore_wait(barrier, n + m - 2)
+
+    og_copies = []
+    for d in range(1, m):
+        copy = pltpu.make_async_remote_copy(
+            src_ref=og,
+            dst_ref=og_rx.at[d - 1],
+            send_sem=og_send.at[d - 1],
+            recv_sem=og_recv.at[d - 1],
+            device_id=(me, lax.rem(col + d, m)),
+            device_id_type=MESH,
+        )
+        copy.start()
+        og_copies.append(copy)
+
+    own_rows = pl.ds(pl.multiple_of(me * cb, cb), cb)
+    sent = {}
+
+    def exchange(part, source, target):
+        place = PARTS.index(part)
+        copies = []
+        for d in range(1, n):
+            peer = lax.rem(me + d, n)
+            copy = pltpu.make_async_remote_copy(
+                src_ref=source(peer),
+                dst_ref=target,
+                send_sem=send.at[place, d - 1],
+                recv_sem=recv.at[place, d - 1],
+                device_id=(peer, col),
+                device_id_type=MESH,
+            )
+            copy.start()
+            copies.append(copy)
+        sent[part] = copies
+
+    def arrived(part):
+        for copy in sent[part]:
+            copy.wait_recv()
+
+    def row_block(peer):
+        return pl.ds(pl.multiple_of(peer * cb, cb), cb)
+
+    tx_prod[...] = (sk[...].astype(F32) * sv[...].astype(F32)).T.astype(BF16)
+    exchange("prod", lambda peer: tx_prod.at[row_block(peer)], rx_prod.at[me])
+    rx_prod[me] = tx_prod[own_rows]
+    for place, gate in enumerate((sq, lk, lf)):
+        tx_gates[place] = flipped(gate[...])
+    exchange("gates", lambda peer: tx_gates.at[:, row_block(peer)], rx_gates.at[me])
+    for place in range(3):
+        rx_gates[me, place] = tx_gates[place, own_rows]
+    filter_t[...] = flipped(sf[...])
+
+    def tiles(k):
+        start = pl.multiple_of(k * kt, kt)
+        return pl.ds(start, kt), pl.ds(pl.multiple_of(seq + start, kt), kt)
+
+    def halves(rows_in, depth, k):
+        cos_at, sin_at = tiles(k)
+        return dot(rows_in, fwd[:depth, cos_at]), dot(rows_in, fwd[:depth, sin_at])
+
+    arrived("prod")
+    for s in range(n):
+        signals[0:cb, s * rows : (s + 1) * rows] = rx_prod[s]
+    loads[1].wait()
+
+    def short_step(k, carry):
+        cos_at, sin_at = tiles(k)
+        pc, ps = halves(signals[0:cb, :], seq, k)
+        fc, fs = halves(filter_t[own_rows, :], taps, k)
+        spec_prod[:, cos_at] = pc
+        spec_prod[:, sin_at] = ps
+        spec_sf[:, cos_at] = fc
+        spec_sf[:, sin_at] = fs
+        waves[0:cb, cos_at] = (pc * fc - ps * fs).astype(BF16)
+        waves[0:cb, sin_at] = (pc * fs + ps * fc).astype(BF16)
+        return carry
+
+    lax.fori_loop(0, seq // kt, short_step, 0)
+    loads[2].wait()
+
+    def at_tokens(step):
+        return pl.ds(pl.multiple_of(step * tile, tile), tile)
+
+    def put(target, step, values):
+        for b in range(2):
+            target[step * 2 + b] = values[:, b * rows : (b + 1) * rows].astype(BF16)
+
+    def short_back(step, carry):
+        mix = dot(waves[0:cb, :], inv[:, at_tokens(step)]) * (1.0 / seq)
+        smix[:, at_tokens(step)] = mix
+        put(tx_smix, step, mix)
+        return carry
+
+    lax.fori_loop(0, n // 2, short_back, 0)
+
+    loads[0].wait()
+    total = jnp.zeros((chans, rows), F32)
+    for d in range(m):
+        if d > 0:
+            og_copies[d - 1].wait_recv()
+        owner = lax.rem(col + m - d, m)
+        features = pl.ds(pl.multiple_of(owner * chans, chans), chans)
+        block = og[...] if d == 0 else og_rx[d - 1]
+        total = total + lax.dot_general(
+            weight_v[:, features], block, (((1,), (1,)), ((), ())), preferred_element_type=F32
+        )
+    grad_out[...] = total.astype(BF16)
+    tx_grad[...] = (
+        total.astype(BF16).astype(F32) * lq[...].astype(F32).T
+    ).astype(BF16)
+    exchange("grad", lambda peer: tx_grad.at[row_block(peer)], rx_grad.at[me])
+    rx_grad[me] = tx_grad[own_rows]
+    exchange("smix", lambda peer: tx_smix.at[peer], smix_out.at[own_rows])
+    smix_out[own_rows, :] = tx_smix[me]
+
+    arrived("gates")
+    for s in range(n):
+        at = slice(s * rows, (s + 1) * rows)
+        mixed = (rx_gates[s, 0].astype(F32) * smix[:, at]).astype(BF16)
+        signals[0:cb, at] = (rx_gates[s, 1].astype(F32) * mixed.astype(F32)).astype(BF16)
+        signals[cb : 2 * cb, at] = rx_gates[s, 2]
+
+    def long_step(k, carry):
+        cos_at, sin_at = tiles(k)
+        c, s = halves(signals[0 : 2 * cb, :], seq, k)
+        spec_u[:, cos_at] = c[0:cb]
+        spec_u[:, sin_at] = s[0:cb]
+        spec_h[:, cos_at] = c[cb:]
+        spec_h[:, sin_at] = s[cb:]
+        waves[0:cb, cos_at] = (c[0:cb] * c[cb:] - s[0:cb] * s[cb:]).astype(BF16)
+        waves[0:cb, sin_at] = (c[0:cb] * s[cb:] + s[0:cb] * c[cb:]).astype(BF16)
+        return carry
+
+    lax.fori_loop(0, seq // kt, long_step, 0)
+
+    arrived("grad")
+    for s in range(n):
+        signals[2 * cb : 3 * cb, s * rows : (s + 1) * rows] = rx_grad[s]
+
+    def grad_step(k, carry):
+        cos_at, sin_at = tiles(k)
+        c, s = halves(signals[2 * cb : 3 * cb, :], seq, k)
+        uc, us = spec_u[:, cos_at], spec_u[:, sin_at]
+        hc, hs = spec_h[:, cos_at], spec_h[:, sin_at]
+        waves[cb : 2 * cb, cos_at] = (hc * c + hs * s).astype(BF16)
+        waves[cb : 2 * cb, sin_at] = (hc * s - hs * c).astype(BF16)
+        waves[2 * cb : 3 * cb, cos_at] = (uc * c + us * s).astype(BF16)
+        waves[2 * cb : 3 * cb, sin_at] = (uc * s - us * c).astype(BF16)
+        return carry
+
+    lax.fori_loop(0, seq // kt, grad_step, 0)
+
+    def long_back(step, carry):
+        mixes = dot(waves[...], inv[:, at_tokens(step)]) * (1.0 / seq)
+        put(tx_lmix, step, mixes[0:cb])
+        put(tx_back, step, mixes[cb : 2 * cb])
+        put(tx_filt, step, mixes[2 * cb :] * (1.0 / math.sqrt(seq)))
+        smix[:, at_tokens(step)] = mixes[cb : 2 * cb]
+        return carry
+
+    lax.fori_loop(0, n // 2, long_back, 0)
+    for part, source, target in (
+        ("back", tx_back, back_out), ("lmix", tx_lmix, lmix_out), ("filt", tx_filt, filt_out)
+    ):
+        exchange(part, lambda peer, source=source: source.at[peer], target.at[own_rows])
+        target[own_rows, :] = source[me]
+
+    for s in range(n):
+        at = slice(s * rows, (s + 1) * rows)
+        mixed_grad = (smix[:, at] * rx_gates[s, 1].astype(F32)).astype(BF16)
+        signals[0:cb, at] = (mixed_grad.astype(F32) * rx_gates[s, 0].astype(F32)).astype(BF16)
+
+    def gate_step(k, carry):
+        cos_at, sin_at = tiles(k)
+        c, s = halves(signals[0:cb, :], seq, k)
+        pc, ps = spec_prod[:, cos_at], spec_prod[:, sin_at]
+        fc, fs = spec_sf[:, cos_at], spec_sf[:, sin_at]
+        waves[0:cb, cos_at] = (fc * c + fs * s).astype(BF16)
+        waves[0:cb, sin_at] = (fc * s - fs * c).astype(BF16)
+        waves[cb : 2 * cb, cos_at] = (pc * c + ps * s).astype(BF16)
+        waves[cb : 2 * cb, sin_at] = (pc * s - ps * c).astype(BF16)
+        return carry
+
+    lax.fori_loop(0, seq // kt, gate_step, 0)
+
+    def short_grad(step, carry):
+        put(tx_bone, step, dot(waves[0:cb, :], inv[:, at_tokens(step)]) * (1.0 / seq))
+        return carry
+
+    lax.fori_loop(0, n // 2, short_grad, 0)
+    exchange("bone", lambda peer: tx_bone.at[peer], bone_out.at[own_rows])
+    bone_out[own_rows, :] = tx_bone[me]
+    terms = dot(waves[cb : 2 * cb, :], inv[:, 0:taps]) * (1.0 / (seq * math.sqrt(seq)))
+    tx_taps[...] = terms.astype(BF16)
+    exchange("taps", lambda peer: tx_taps, taps_out.at[own_rows])
+    taps_out[own_rows, :] = tx_taps[...]
+
+    for part in PARTS[3:]:
+        arrived(part)
+    for part in PARTS:
+        for copy in sent[part]:
+            copy.wait_send()
+    for copy in og_copies:
+        copy.wait_send()
+
+
+def finish_kernel(
+    grad, smix, lmix, filt, back, bone, taps, sq, sk, sv, lk,
+    sq_grad, sk_grad, sv_grad, sf_grad, lq_grad, lk_grad, lf_grad,
+):
+    def turned(ref):
+        return ref[...].astype(F32).T
+
+    short_mix, back_two, back_one = turned(smix), turned(back), turned(bone)
+    mixed = (sq[...].astype(F32) * short_mix).astype(BF16).astype(F32)
+    mixed_grad = (back_two * lk[...].astype(F32)).astype(BF16).astype(F32)
+    sq_grad[...] = (mixed_grad * short_mix).astype(BF16)
+    lk_grad[...] = (back_two * mixed).astype(BF16)
+    sk_grad[...] = (back_one * sv[...].astype(F32)).astype(BF16)
+    sv_grad[...] = (back_one * sk[...].astype(F32)).astype(BF16)
+    lq_grad[...] = (turned(grad) * turned(lmix)).astype(BF16)
+    lf_grad[...] = turned(filt).astype(BF16)
+    sf_grad[...] = turned(taps).astype(BF16)
+
+
+def dense_body(
+    n, m, sq, sk, sv, sf, lq, lk, lf, weight, og
+):
+    rows, chans = sq.shape
+    taps = sf.shape[0]
+    seq = rows * n
+    cb = chans // n
+    forward, inverse = wave_tables(seq)
+    vmem = pl.BlockSpec(memory_space=pltpu.VMEM)
+    hbm = pl.BlockSpec(memory_space=pl.ANY)
+    turned = jax.ShapeDtypeStruct((chans, rows), BF16)
+    blocks = pltpu.VMEM((n, cb, rows), BF16)
+    spectrum = pltpu.VMEM((cb, 2 * seq), F32)
+    moved = pl.pallas_call(
+        functools.partial(operator_kernel, n, m),
+        out_shape=[turned] * 6 + [jax.ShapeDtypeStruct((chans, taps), BF16)],
+        in_specs=[vmem] * 8 + [hbm] * 3,
+        out_specs=[vmem] * 7,
+        scratch_shapes=[
+            pltpu.VMEM(weight.shape, BF16),
+            pltpu.VMEM(forward.shape, BF16),
+            pltpu.VMEM(inverse.shape, BF16),
+            pltpu.VMEM((m - 1, rows, chans), BF16),
+            pltpu.VMEM((chans, rows), BF16),
+            pltpu.VMEM((3, chans, rows), BF16),
+            pltpu.VMEM((chans, rows), BF16),
+            blocks,
+            pltpu.VMEM((n, 3, cb, rows), BF16),
+            blocks,
+            blocks, blocks, blocks, blocks, blocks,
+            pltpu.VMEM((cb, taps), BF16),
+            pltpu.VMEM((chans, taps), BF16),
+            pltpu.VMEM((3 * cb, seq), BF16),
+            pltpu.VMEM((cb, seq), F32),
+            spectrum, spectrum, spectrum, spectrum,
+            pltpu.VMEM((3 * cb, 2 * seq), BF16),
+            pltpu.SemaphoreType.DMA((3,)),
+            pltpu.SemaphoreType.DMA((m - 1,)),
+            pltpu.SemaphoreType.DMA((m - 1,)),
+            pltpu.SemaphoreType.DMA((len(PARTS), n - 1)),
+            pltpu.SemaphoreType.DMA((len(PARTS), n - 1)),
+        ],
+        compiler_params=pltpu.CompilerParams(
+            collective_id=0, has_side_effects=True, vmem_limit_bytes=40 * 1024 * 1024
+        ),
+    )(sq, sk, sv, sf, lq, lk, lf, og, weight, jnp.asarray(forward), jnp.asarray(inverse))
+    tokens = jax.ShapeDtypeStruct((rows, chans), BF16)
+    return pl.pallas_call(
+        finish_kernel,
+        out_shape=[tokens] * 3 + [jax.ShapeDtypeStruct((taps, chans), BF16)] + [tokens] * 3,
+        in_specs=[vmem] * 11,
+        out_specs=[vmem] * 7,
+        compiler_params=pltpu.CompilerParams(vmem_limit_bytes=24 * 1024 * 1024),
+    )(*moved, sq, sk, sv, lk)
+
+
+def body(n, m, *arrays):
+    rows, chans = arrays[0].shape
+    taps = arrays[3].shape[0]
+    dense = (
+        rows * n <= LONGEST_DENSE
+        and rows % 128 == 0
+        and taps % 128 == 0
+        and taps <= rows * n
+        and n > 1
+        and n % 2 == 0
+        and m > 1
+        and chans % (16 * n) == 0
+        and chans % 128 == 0
+    )
+    if dense:
+        return tuple(dense_body(n, m, *arrays))
+    return general_body(*arrays)
+
+
 def solution(mesh):
     in_specs = (
         P("ctx", "tp"),
@@ -232,4 +594,5 @@
         P("ctx", "tp"),
         P("ctx", "tp"),
     )
-    return jax.shard_map(body, mesh=mesh, in_specs=in_specs, out_specs=out_specs, check_vma=False)
+    return jax.shard_map(
+        functools.partial(body, mesh.shape["ctx"], mesh.shape["tp"]), mesh=mesh, in_specs=in_specs, out_specs=out_specs, check_vma=False)

time: 288 us -> 57.6 us (0.20); the launches traced: 284 us -> 57.3 us
  other arithmetic: 68.9 us -> 0 us
  waiting for transfers between devices: 59.1 us -> 0 us
  Pallas kernels: 0 us -> 43.4 us
  local copies, waits for them, and re-layouts: 53.9 us -> 13.2 us
  starting transfers between devices: 33.1 us -> 0 us
  matrix products: 31.8 us -> 0 us
  loops' own time: 15.7 us -> 0 us
  between operations: 14.6 us -> 0.66 us
  blocking collectives: 7.37 us -> 0 us
    pallas_call x0 -> x2, Pallas kernels: none -> 43.4 us  [the longest x1 42.3 us: dense_body(): pl.pallas_call(functools.partial(operator_kernel, n, m), out_shape=[turne...]
    psum x1 -> x0, waiting for transfers between devices: 35.3 us -> none  [body(): filter_one = lax.psum(local_terms, 'ctx')]
    mul x32 -> x0, other arithmetic: 32.7 us -> none  [group_step(): total = total + weight_row[None, :] * shifted]
    dot_general x33 -> x0, matrix products: 31.8 us -> none  [the longest x3 4.73 us: spectrum(): imag_a = -jnp.einsum('kn,ncm->kcm', sin_one, values, precision=highest)]
    all_to_all x6 -> x0, starting transfers between devices: 26.2 us -> none  [the longest x1 5.99 us: body(): lax.all_to_all(to_channels(long_filter), 'ctx', split_axis=0, concat_axis...]
    all_to_all x6 -> x0, waiting for transfers between devices: 21.5 us -> none  [the longest x1 6.3 us: body(): lax.all_to_all(conv_part, 'ctx', split_axis=0, concat_axis=0, tiled=True)]
    dynamic_slice x16 -> x0, local copies, waits for them, and re-layouts: 18.9 us -> none  [filter_terms(): lax.map(group_terms, jnp.arange(filter_taps // 8, dtype=jnp.int32))]
    reduce_sum x16 -> x0, other arithmetic: 15.9 us -> none  [group_terms(): partials.append(jnp.sum(grads * shifted, axis=0))]
  transfers between devices with their start and end apart: 9 -> 0, of which waited for: 7 -> 0; matrix products, arithmetic and copies ran while one was open for 25% -> 0% of each run, Pallas kernels for 0% -> 0%
where the time goes in v1:
time: 57.6 us; the launch traced here: 57.3 us
  Pallas kernels  43.4 us (75%)
  local copies, waits for them, and re-layouts  13.2 us (23%)
  between operations  0.66 us (1%)
    pallas_call x1, Pallas kernels, dense_body(): pl.pallas_call(functools.partial(operator_kernel, n, m), out_shape=[turne...  42.3 us
    unnamed x22, local copies, waits for them, and re-layouts  13.2 us
    pallas_call x1, Pallas kernels, dense_body(): pl.pallas_call(finish_kernel, out_shape=[tokens] * 3 + [jax.ShapeDtypeStr...  1.17 us

profile of v1, /device:TPU:0, one launch (start us, length us, event | category | flops | bytes accessed | tf_op | source)
XLA Modules:
  0.0 57.3 jit_solution(9233159562618628252)
XLA Ops:
  0.6 0.0 copy-start
  0.6 2.2 %copy-done = bf16[2048,1024]{1,0:T(8,128)(2,1)S(1)} copy-done((bf16[2048,1024]{1,0:T(8,128)(2,1)S(1)}, bf16[2048,1024]{1,0:T(8,128)(2,1)}, u32[]{:S(2)}) %copy-start) | copy-done | bytes 4194328
  2.8 0.0 copy-start.1
  2.8 2.2 %copy-done.1 = bf16[1024,2048]{1,0:T(8,128)(2,1)S(1)} copy-done((bf16[1024,2048]{1,0:T(8,128)(2,1)S(1)}, bf16[1024,2048]{1,0:T(8,128)(2,1)}, u32[]{:S(2)}) %copy-start.1) | copy-done | bytes 4194328
  5.0 0.0 copy-start.2
  5.0 1.6 %copy-done.2 = bf16[512,2048]{1,0:T(8,128)(2,1)S(1)} copy-done((bf16[512,2048]{1,0:T(8,128)(2,1)S(1)}, bf16[512,2048]{1,0:T(8,128)(2,1)}, u32[]{:S(2)}) %copy-start.2) | copy-done | bytes 2097176
  6.6 0.0 copy-start.3
  6.6 0.9 %copy-done.3 = bf16[128,512]{1,0:T(8,128)(2,1)S(1)} copy-done((bf16[128,512]{1,0:T(8,128)(2,1)S(1)}, bf16[128,512]{1,0:T(8,128)(2,1)}, u32[]{:S(2)}) %copy-start.3) | copy-done | bytes 131096
  7.5 0.0 copy-start.4
  7.5 0.9 %copy-done.4 = bf16[128,512]{1,0:T(8,128)(2,1)S(1)} copy-done((bf16[128,512]{1,0:T(8,128)(2,1)S(1)}, bf16[128,512]{1,0:T(8,128)(2,1)}, u32[]{:S(2)}) %copy-start.4) | copy-done | bytes 131096
  8.4 0.0 copy-start.5
  8.4 0.9 %copy-done.5 = bf16[128,512]{1,0:T(8,128)(2,1)S(1)} copy-done((bf16[128,512]{1,0:T(8,128)(2,1)S(1)}, bf16[128,512]{1,0:T(8,128)(2,1)}, u32[]{:S(2)}) %copy-start.5) | copy-done | bytes 131096
  9.3 0.0 copy-start.6
  9.3 0.9 %copy-done.6 = bf16[128,512]{1,0:T(8,128)(2,1)S(1)} copy-done((bf16[128,512]{1,0:T(8,128)(2,1)S(1)}, bf16[128,512]{1,0:T(8,128)(2,1)}, u32[]{:S(2)}) %copy-start.6) | copy-done | bytes 131096
  10.2 0.0 copy-start.7
  10.2 0.9 %copy-done.7 = bf16[128,512]{1,0:T(8,128)(2,1)S(1)} copy-done((bf16[128,512]{1,0:T(8,128)(2,1)S(1)}, bf16[128,512]{1,0:T(8,128)(2,1)}, u32[]{:S(2)}) %copy-start.7) | copy-done | bytes 131096
  11.1 0.0 copy-start.8
  11.1 0.9 %copy-done.8 = bf16[128,512]{1,0:T(8,128)(2,1)S(1)} copy-done((bf16[128,512]{1,0:T(8,128)(2,1)S(1)}, bf16[128,512]{1,0:T(8,128)(2,1)}, u32[]{:S(2)}) %copy-start.8) | copy-done | bytes 131096
  12.0 0.0 copy-start.9
  12.0 0.9 %copy-done.9 = bf16[128,512]{1,0:T(8,128)(2,1)S(1)} copy-done((bf16[128,512]{1,0:T(8,128)(2,1)S(1)}, bf16[128,512]{1,0:T(8,128)(2,1)}, u32[]{:S(2)}) %copy-start.9) | copy-done | bytes 131096
  12.9 0.0 copy-start.10
  12.9 0.9 %copy-done.10 = bf16[128,512]{1,0:T(8,128)(2,1)S(1)} copy-done((bf16[128,512]{1,0:T(8,128)(2,1)S(1)}, bf16[128,512]{1,0:T(8,128)(2,1)}, u32[]{:S(2)}) %copy-start.10) | copy-done | bytes 131096
  13.8 42.3 %shard_map.162 = (bf16[512,128]{1,0:T(8,128)(2,1)S(1)}, bf16[512,128]{1,0:T(8,128)(2,1)S(1)}, bf16[512,128]{1,0:T(8,128)(2,1)S(1)}, bf16[512,128]{1,0:T(8,128)(2...) custom-call(bf16[128,512]{1,0:T(8,128)(2,1)S(1)} %copy-done.3, ...), custom_call_target="tpu_custom_call" | custom-call | tf_op jit(solution)/shard_map/pallas_call | solution.py:514
  56.1 1.2 %shard_map.163 = (bf16[128,512]{1,0:T(8,128)(2,1)}, bf16[128,512]{1,0:T(8,128)(2,1)}, bf16[128,512]{1,0:T(8,128)(2,1)}, bf16[128,512]{1,0:T(8,128)(2,1)}, bf16[1...) custom-call(bf16[512,128]{1,0:T(8,128)(2,1)S(1)} %get-tuple-element.14.grad, ...), custom_call_target="tpu_custom_call" | custom-call | tf_op jit(solution)/shard_map/pallas_call | solution.py:548
Async XLA Ops:
  0.6 2.2 %copy-start = (bf16[2048,1024]{1,0:T(8,128)(2,1)S(1)}, bf16[2048,1024]{1,0:T(8,128)(2,1)}, u32[]{:S(2)}) copy-start(bf16[2048,1024]{1,0:T(8,128)(2,1)} %constant.5.clone.inverse) | copy-start | bytes 12582916
  2.8 2.2 %copy-start.1 = (bf16[1024,2048]{1,0:T(8,128)(2,1)S(1)}, bf16[1024,2048]{1,0:T(8,128)(2,1)}, u32[]{:S(2)}) copy-start(bf16[1024,2048]{1,0:T(8,128)(2,1)} %constant.4.clone.forward) | copy-start | bytes 12582916
  5.0 1.6 %copy-start.2 = (bf16[512,2048]{1,0:T(8,128)(2,1)S(1)}, bf16[512,2048]{1,0:T(8,128)(2,1)}, u32[]{:S(2)}) copy-start(bf16[512,2048]{1,0:T(8,128)(2,1)} %weight.1) | copy-start | bytes 6291460
  6.6 0.9 %copy-start.3 = (bf16[128,512]{1,0:T(8,128)(2,1)S(1)}, bf16[128,512]{1,0:T(8,128)(2,1)}, u32[]{:S(2)}) copy-start(bf16[128,512]{1,0:T(8,128)(2,1)} %sq.3) | copy-start | bytes 393220
  7.5 0.9 %copy-start.4 = (bf16[128,512]{1,0:T(8,128)(2,1)S(1)}, bf16[128,512]{1,0:T(8,128)(2,1)}, u32[]{:S(2)}) copy-start(bf16[128,512]{1,0:T(8,128)(2,1)} %sk.3) | copy-start | bytes 393220
  8.4 0.9 %copy-start.5 = (bf16[128,512]{1,0:T(8,128)(2,1)S(1)}, bf16[128,512]{1,0:T(8,128)(2,1)}, u32[]{:S(2)}) copy-start(bf16[128,512]{1,0:T(8,128)(2,1)} %sv.3) | copy-start | bytes 393220
  9.3 0.9 %copy-start.6 = (bf16[128,512]{1,0:T(8,128)(2,1)S(1)}, bf16[128,512]{1,0:T(8,128)(2,1)}, u32[]{:S(2)}) copy-start(bf16[128,512]{1,0:T(8,128)(2,1)} %lk.3) | copy-start | bytes 393220
  10.2 0.9 %copy-start.7 = (bf16[128,512]{1,0:T(8,128)(2,1)S(1)}, bf16[128,512]{1,0:T(8,128)(2,1)}, u32[]{:S(2)}) copy-start(bf16[128,512]{1,0:T(8,128)(2,1)} %sf.1) | copy-start | bytes 393220
  11.1 0.9 %copy-start.8 = (bf16[128,512]{1,0:T(8,128)(2,1)S(1)}, bf16[128,512]{1,0:T(8,128)(2,1)}, u32[]{:S(2)}) copy-start(bf16[128,512]{1,0:T(8,128)(2,1)} %lq.1) | copy-start | bytes 393220
  12.0 0.9 %copy-start.9 = (bf16[128,512]{1,0:T(8,128)(2,1)S(1)}, bf16[128,512]{1,0:T(8,128)(2,1)}, u32[]{:S(2)}) copy-start(bf16[128,512]{1,0:T(8,128)(2,1)} %lf.1) | copy-start | bytes 393220
  12.9 0.9 %copy-start.10 = (bf16[128,512]{1,0:T(8,128)(2,1)S(1)}, bf16[128,512]{1,0:T(8,128)(2,1)}, u32[]{:S(2)}) copy-start(bf16[128,512]{1,0:T(8,128)(2,1)} %og.1) | copy-start | bytes 393220
